TPU v7x, 256 devices: a whole 4x4x8 slice. The times are simulated.
256 devices in a mesh: ia: 8 (over z), ja: 32 (over x, y, core).
Axes of the slice: x: 4, y: 4, z: 8, core: 2. Of those that a mesh axis runs over, the one named last changes fastest.
Arguments:
- tensor: float32 [8, 8192, 8192], P(None, 'ia', 'ja'), may hold values from -6 to 6
- factor_b: float32 [8192, 256], P(('ja', 'ia')), may hold values from -24 to 24, as said below
- factor_c: float32 [8, 256], replicated, may hold values from -0.0234375 to 0.0234375
Outputs:
- factor_a: float32 [8192, 256], P(('ia', 'ja'))
- factor_b_new: float32 [8192, 256], P(('ja', 'ia'))
Inputs may be any that keep to these rules, and one draw needn't show every extreme that they name: `factor_b`: real-valued entries.
All inputs are finite; a program needn't handle non-finite values.
Results may differ from a plain program's by a relative error of at most 0.0001.
Values sent between devices are 32-bit elements; how exact they have to be, the bound alone decides.
A program may use at most 64 MiB of HBM per device.

v0:
```python
import jax
import jax.numpy as jnp
from jax import lax
from jax.sharding import PartitionSpec as P

RIDGE = 0.001


def cross(left, right):
    return lax.dot_general(
        left,
        right,
        (((0,), (0,)), ((), ())),
        precision=lax.Precision.HIGHEST,
        preferred_element_type=jnp.float32,
    )


def solve_rows(moments, gram_c, gram_other):
    size = gram_c.shape[0]
    system = gram_c * gram_other + RIDGE * jnp.eye(size, dtype=jnp.float32)
    lower = jnp.linalg.cholesky(system)
    middle = lax.linalg.triangular_solve(
        lower, moments, left_side=False, lower=True, transpose_a=True
    )
    return lax.linalg.triangular_solve(
        lower, middle, left_side=False, lower=True, transpose_a=False
    )


def local(tensor, factor_b, factor_c):
    highest = lax.Precision.HIGHEST
    gram_c = cross(factor_c, factor_c)
    slab = tensor
    weighted = lax.all_gather(factor_b, "ia", axis=0, tiled=True)[None, :, :] * factor_c[:, None, :]
    total = jnp.einsum(
        "kin,knr->ir", slab, weighted, precision=highest, preferred_element_type=jnp.float32
    )
    gram_b = lax.psum(cross(factor_b, factor_b), ("ia", "ja"))
    moments_owned = lax.psum_scatter(total, "ja", scatter_dimension=0, tiled=True)
    factor_a = solve_rows(moments_owned, gram_c, gram_b)
    slab = tensor
    weighted = lax.all_gather(factor_a, "ja", axis=0, tiled=True)[None, :, :] * factor_c[:, None, :]
    total = jnp.einsum(
        "knj,knr->jr", slab, weighted, precision=highest, preferred_element_type=jnp.float32
    )
    gram_a = lax.psum(cross(factor_a, factor_a), ("ia", "ja"))
    moments_b_owned = lax.psum_scatter(total, "ia", scatter_dimension=0, tiled=True)
    factor_b_new = solve_rows(moments_b_owned, gram_c, gram_a)
    return (factor_a, factor_b_new)


def solution(mesh):
    in_specs = (P(None, "ia", "ja"), P(("ja", "ia"), None), P())
    out_specs = (P(("ia", "ja"), None), P(("ja", "ia"), None))
    return jax.shard_map(local, mesh=mesh, in_specs=in_specs, out_specs=out_specs, check_vma=False)
```

profile of v0, /device:TPU:1, one launch (start us, length us, event | category | flops | bytes accessed | tf_op | source)
XLA Modules:
  0.0 682.6 jit_solution(7424416333277194527)
XLA Ops:
  8.1 2.0 fusion.38
  10.1 23.5 %all_gather.6 = f32[256,256]{1,0:T(8,128)S(1)} all-gather(f32[32,256]{1,0:T(8,128)} %param.9), channel_id=1, replica_groups=mesh['ia'=8,'ja'=32] {'ia'}, dimensions={0}, use_global_device_ids=true | all-gather | bytes 294912 | tf_op jit(solution)/shard_map/all_gather | solution.py:35
  33.7 9.9 %fusion.6 = f32[1024,256]{0,1:T(8,128)S(1)} fusion(f32[8,1024,256]{2,1,0:T(8,128)} %param.8, f32[8,256]{1,0:T(8,128)} %param.10, f32[256,256]{0,1:T(8,128)S(1)} %copy.16), kind=kOutput, calls=%fused_computation.10 | convolution fusion | flops 6442975232 | bytes 9707520 | tf_op jit(solution)/shard_map/kin,knr->ir/dot_general | solution.py:36
  43.7 1.3 copy.24
  45.5 222.3 %all-reduce.4.cloned.1.call-done = f32[256,256]{0,1:T(8,128)} async-done(((f32[256,256]{0,1:T(8,128)}), f32[256,256]{0,1:T(8,128)}) %all-reduce.4.cloned.1.call-update) | async-done | bytes 262160 | tf_op jit(solution)/shard_map/psum | solution.py:39
  267.8 1.4 select_add_fusion.1
  269.4 11.7 %cholesky.130 = f32[128,128]{1,0:T(8,128)S(1)} custom-call(f32[128,128]{1,0:T(8,128)S(1)} %cholesky.194), custom_call_target="Cholesky" | custom-call | tf_op jit(solution)/shard_map/jit(cholesky)/cholesky | solution.py:22
  281.2 9.8 %custom-call.17 = f32[1,128,128]{1,2,0:T(8,128)S(1)} custom-call(f32[1,128,128]{2,1,0:T(8,128)S(1)} %get-tuple-element.64), custom_call_target="InvertDiagBlocksLowerTriangular" | custom-call | tf_op jit(solution)/shard_map/jit(cholesky)/cholesky | solution.py:22
  291.5 11.7 %cholesky.147 = f32[128,128]{1,0:T(8,128)S(1)} custom-call(f32[128,128]{1,0:T(8,128)S(1)} %convolution_subtract_fusion.3), custom_call_target="Cholesky" | custom-call | tf_op jit(solution)/shard_map/jit(cholesky)/cholesky | solution.py:22
  305.3 4.2 while.8
  306.2 1.3 bitcast_dynamic-update-slice_fusion.4
  308.2 1.3 bitcast_dynamic-update-slice_fusion.4
  309.5 19.7 %custom-call.18 = f32[2,128,128]{1,2,0:T(8,128)S(1)} custom-call(f32[2,128,128]{2,1,0:T(8,128)S(1)} %get-tuple-element.33), custom_call_target="InvertDiagBlocksLowerTriangular" | custom-call | tf_op jit(solution)/shard_map/triangular_solve/custom-call.0 | solution.py:23
  333.9 249.0 %all-reduce.6.cloned.1.call-done = f32[256,256]{0,1:T(8,128)} async-done(((f32[256,256]{0,1:T(8,128)}), f32[256,256]{0,1:T(8,128)}) %all-reduce.6.cloned.1.call-update) | async-done | bytes 262160 | tf_op jit(solution)/shard_map/psum | solution.py:47
  584.1 11.7 %cholesky.164 = f32[128,128]{1,0:T(8,128)S(1)} custom-call(f32[128,128]{1,0:T(8,128)S(1)} %cholesky.197), custom_call_target="Cholesky" | custom-call | tf_op jit(solution)/shard_map/jit(cholesky)/cholesky | solution.py:22
  595.9 9.8 %custom-call.20 = f32[1,128,128]{1,2,0:T(8,128)S(1)} custom-call(f32[1,128,128]{2,1,0:T(8,128)S(1)} %get-tuple-element.60), custom_call_target="InvertDiagBlocksLowerTriangular" | custom-call | tf_op jit(solution)/shard_map/jit(cholesky)/cholesky | solution.py:22
  606.2 11.7 %cholesky.181 = f32[128,128]{1,0:T(8,128)S(1)} custom-call(f32[128,128]{1,0:T(8,128)S(1)} %convolution_subtract_fusion.1), custom_call_target="Cholesky" | custom-call | tf_op jit(solution)/shard_map/jit(cholesky)/cholesky | solution.py:22
  620.6 1.6 copy.20
  622.2 16.6 %fusion.9 = f32[256,256]{0,1:T(8,128)S(1)} fusion(f32[8,1024,256]{2,1,0:T(8,128)} %param.8, f32[8,256]{1,0:T(8,128)S(1)} %copy-done.1, f32[1024,256]{0,1:T(8,128)S(1)} %copy.20), kind=kOutput, calls=%fused_computation.11 | convolution fusion | flops 6444548096 | bytes 9707520 | tf_op jit(solution)/shard_map/knj,knr->jr/dot_general | solution.py:44
  639.6 3.9 while.9
  640.3 1.3 bitcast_dynamic-update-slice_fusion.5
  642.2 1.3 bitcast_dynamic-update-slice_fusion.5
  643.5 19.7 %custom-call.21 = f32[2,128,128]{1,2,0:T(8,128)S(1)} custom-call(f32[2,128,128]{2,1,0:T(8,128)S(1)} %get-tuple-element.35), custom_call_target="InvertDiagBlocksLowerTriangular" | custom-call | tf_op jit(solution)/shard_map/triangular_solve/custom-call.0 | solution.py:23
  663.2 8.6 %reduce-scatter.9.cloned.1.call-done = f32[32,256]{1,0:T(8,128)} async-done(((f32[256,256]{1,0:T(8,128)}), f32[32,256]{1,0:T(8,128)}) %reduce-scatter.9.cloned.1.call-update) | async-done | bytes 32784
  (71 shorter events, 16.8 us)
Async XLA Ops:
  8.0 259.8 %copy-start.1 = (f32[8,256]{1,0:T(8,128)S(1)}, f32[8,256]{1,0:T(8,128)}, u32[]{:S(2)}) copy-start(f32[8,256]{1,0:T(8,128)} %param.10) | copy-start | bytes 24580
  8.0 259.8 %all-reduce.4.cloned.1.call-start = ((), (), s32[]{:S(2)}) async-start(), calls=%async_computation.2 | async-start | bytes 524288 | tf_op jit(solution)/shard_map/psum | solution.py:39
  10.0 319.2 %reduce-scatter.7.cloned.1.call-start = ((), (), s32[]{:S(2)}) async-start(), calls=%async_computation.5 | async-start | bytes 1081344
  45.0 537.9 %all-reduce.6.cloned.1.call-start = ((), (), s32[]{:S(2)}) async-start(), calls=%async_computation.3 | async-start | bytes 524288 | tf_op jit(solution)/shard_map/psum | solution.py:47
  332.1 1.2 copy-start
  333.3 287.4 %all-gather.2.cloned.1.call-start = ((), (), s32[]{:S(2)}) async-start(), calls=%async_computation.4 | async-start | bytes 1081344 | tf_op jit(solution)/shard_map/all_gather | solution.py:43
  333.9 338.0 %reduce-scatter.9.cloned.1.call-start = ((), (), s32[]{:S(2)}) async-start(), calls=%async_computation.6 | async-start | bytes 294912
Sparse Core Ops, SparseCore 0:
  15.2 252.5 all-reduce.3
  333.4 249.4 all-reduce.5
  639.7 32.0 reduce-scatter.8
Sparse Core Ops, SparseCore 1:
  45.1 88.8 reduce-scatter.6
  337.2 48.4 all-gather.1
where the time goes:
time: 691 us; the launch traced here: 683 us
  waiting for transfers between devices  481 us (70%)
  other arithmetic  110 us (16%)
  matrix products  35.7 us (5%)
  blocking collectives  23.5 us (3%)
  between operations  18.3 us (3%)
  local copies, waits for them, and re-layouts  13.7 us (2%)
    psum x1, waiting for transfers between devices, local(): gram_a = lax.psum(cross(factor_a, factor_a), ('ia', 'ja'))  249 us
    psum x1, waiting for transfers between devices, local(): gram_b = lax.psum(cross(factor_b, factor_b), ('ia', 'ja'))  222 us
    another operation x13, other arithmetic, solve_rows(): lower = jnp.linalg.cholesky(system)  68.7 us
    another operation x5, other arithmetic, solve_rows(): lax.linalg.triangular_solve(lower, moments, left_side=False, lower=True,...  39.4 us
    all_gather x1, blocking collectives, local(): lax.all_gather(factor_b, 'ia', axis=0, tiled=True)[None, :, :]  23.5 us
    dot_general x1, matrix products, local(): jnp.einsum('knj,knr->jr', slab, weighted, precision=highest, preferred_el...  16.6 us
  transfers between devices with their start and end apart: 5, of which 3 were waited for; matrix products, arithmetic and copies ran while one was open for 19% of the time, Pallas kernels for 0%

commit v1 on v0

v1 whole, which is shorter than its diff:
```python
import functools

import jax
import jax.numpy as jnp
from jax import lax
from jax.experimental import pallas as pl
from jax.experimental.pallas import tpu as pltpu
from jax.sharding import PartitionSpec as P

RIDGE = 0.001
MESH = pl.DeviceIdType.MESH
F32 = jnp.float32
BF16 = jnp.bfloat16
PB = 16
CHUNKS = 4


def split2(x):
    high = x.astype(BF16)
    return high, (x - high.astype(F32)).astype(BF16)


def split3(x):
    high = x.astype(BF16)
    rest = x - high.astype(F32)
    mid = rest.astype(BF16)
    return high, mid, (rest - mid.astype(F32)).astype(BF16)


def cross(left, right):
    lh, lm, ll = split3(left)
    rh, rm, rl = split3(right)
    a = jnp.concatenate([lh, lh, lm, lh, lm, ll], axis=0)
    b = jnp.concatenate([rh, rm, rh, rl, rm, rh], axis=0)
    return lax.dot_general(a, b, (((0,), (0,)), ((), ())), preferred_element_type=F32)


def row_of(block, at):
    return jnp.broadcast_to(block[at : at + 1, :], block.shape)


def sweep_small(cols, width):
    row = lax.broadcasted_iota(jnp.int32, (8, width), 0)
    halves = range(PB // 8)
    for j in range(0, PB, 2):
        h, jj = j // 8, j % 8
        u0, u1 = cols[j], cols[j + 1]
        first, second = row == jj, row == jj + 1
        a, b, d = row_of(u0[h], jj), row_of(u0[h], jj + 1), row_of(u1[h], jj + 1)
        scale = 1.0 / (a * d - b * b)
        p00, p01, p11 = d * scale, -b * scale, a * scale
        fresh = []
        for l in range(PB):
            if l == j or l == j + 1:
                r0, r1 = (p00, p01) if l == j else (p01, p11)
                col = [u0[g] * r0 + u1[g] * r1 for g in halves]
                r0, r1 = -r0, -r1
            else:
                q0, q1 = row_of(cols[l][h], jj), row_of(cols[l][h], jj + 1)
                r0, r1 = p00 * q0 + p01 * q1, p01 * q0 + p11 * q1
                col = [cols[l][g] - u0[g] * r0 - u1[g] * r1 for g in halves]
            col[h] = jnp.where(first, r0, jnp.where(second, r1, col[h]))
            fresh.append(col)
        cols = fresh
    return cols


def sweep(s_ref):
    size = s_ref.shape[0]
    lanes = lax.broadcasted_iota(jnp.int32, (PB, size), 1)
    rows = lax.broadcasted_iota(jnp.int32, (PB, size), 0)
    width = 128

    def step(k, carry):
        at = pl.multiple_of(k * PB, PB)
        panel = s_ref[pl.ds(at, PB), :]
        cols = []
        for l in range(PB):
            col = jnp.sum(jnp.where(lanes == at + l, panel, 0.0), axis=1, keepdims=True)
            col = jnp.broadcast_to(col, (PB, width))
            cols.append([col[8 * g : 8 * g + 8] for g in range(PB // 8)])
        cols = sweep_small(cols, width)
        inside = (lanes >= at) & (lanes < at + PB)
        source = jnp.where(inside, jnp.where(lanes == at + rows, 1.0, 0.0), -panel)
        parts = [[None] * (size // width) for _ in range(PB // 8)]
        for l in range(PB):
            for w in range(size // width):
                line = jnp.broadcast_to(source[l : l + 1, w * width : (w + 1) * width], (8, width))
                for g in range(PB // 8):
                    term = cols[l][g] * line
                    parts[g][w] = term if l == 0 else parts[g][w] + term
        fresh = jnp.concatenate([jnp.concatenate(p, axis=1) for p in parts], axis=0)
        update = cross(panel, fresh)
        whole = lax.broadcasted_iota(jnp.int32, (size, size), 1)
        kept = jnp.where((whole >= at) & (whole < at + PB), 0.0, s_ref[...])
        s_ref[...] = kept - update
        s_ref[pl.ds(at, PB), :] = fresh
        return carry

    lax.fori_loop(0, size // PB, step, 0)


def dot(a, b):
    return jnp.dot(a, b, preferred_element_type=F32)


def full_dot(a, b):
    return jnp.dot(a, b, precision=lax.Precision.HIGHEST, preferred_element_type=F32)


def kernel(nz, nj, t_hbm, b_ref, c_ref, fa_ref, fb_ref,
           t_f32, t_hi, t_lo, w_hi, w_lo, b_all, c_pad, c_turn, gram_c,
           gram, g1, g1_sum, g2, g2_sum, g3, system,
           tot, sib, comb, landed, a_all, at_hi, at_lo, tot_b, h_land,
           t_sem, a_s, a_r, g1_s, g1_r, g2_s, g2_r, g3_s, g3_r, c1_s, c1_r, c2_s, c2_r, e1_s, e2_s, e_r, h_s, h_r):
    z, p = lax.axis_index("ia"), lax.axis_index("ja")
    q, c = p // 2, p % 2
    nq = nj // 2
    per = b_ref.shape[0]
    rank = b_ref.shape[1]
    layers = t_hbm.shape[0]
    high = t_hbm.shape[1]
    wide = t_hbm.shape[2]
    slab = rank // nj
    other = p + 1 - 2 * c

    def send(src, dst, s_sem, r_sem, to):
        return pltpu.make_async_remote_copy(
            src_ref=src, dst_ref=dst, send_sem=s_sem, recv_sem=r_sem, device_id=to, device_id_type=MESH
        )

    def each(n, body):
        lax.fori_loop(0, n, lambda s, carry: (body(s), carry)[1], 0)

    t_copies = [pltpu.make_async_copy(t_hbm.at[k], t_f32.at[k], t_sem.at[k]) for k in range(layers)]
    for copy in t_copies:
        copy.start()

    barrier = pltpu.get_barrier_semaphore()
    each(nj - 1, lambda s: pl.semaphore_signal(
        barrier, inc=1, device_id=(z, (p + 1 + s) % nj), device_id_type=MESH))
    each(nz - 1, lambda s: pl.semaphore_signal(
        barrier, inc=1, device_id=((z + 1 + s) % nz, p), device_id_type=MESH))

    def g1_copy(t, to, slot):
        return send(gram.at[t, to], g1.at[t, slot], g1_s.at[t, to], g1_r.at[t, slot], (z, to))

    def g2_copy(t, to, slot):
        return send(g1_sum.at[t], g2.at[t, slot], g2_s.at[t, to], g2_r.at[t, slot], (to, p))

    def g3_copy(t, to, slot):
        return send(g2_sum.at[t], g3.at[t, slot], g3_s.at[t, to], g3_r.at[t, slot], (z, to))

    def gram_local(t, rows):
        gram[t] = cross(rows, rows).reshape(nj, slab, rank)

    def gram_1(t):
        each(nj - 1, lambda s: g1_copy(t, (p + 1 + s) % nj, p).start())

    def gram_2(t):
        g1[t, p] = gram[t, p]
        each(nj - 1, lambda s: g1_copy(t, p, (p + 1 + s) % nj).wait_recv())
        total = g1[t, 0]
        for s in range(1, nj):
            total = total + g1[t, s]
        g1_sum[t] = total
        each(nz - 1, lambda s: g2_copy(t, (z + 1 + s) % nz, z).start())
        g2[t, z] = total

    def gram_3(t):
        each(nz - 1, lambda s: g2_copy(t, z, (z + 1 + s) % nz).wait_recv())
        total = g2[t, 0]
        for s in range(1, nz):
            total = total + g2[t, s]
        g2_sum[t] = total
        each(nj - 1, lambda s: g3_copy(t, (p + 1 + s) % nj, p).start())
        g3[t, p] = total

    def gram_4(t):
        each(nj - 1, lambda s: g3_copy(t, p, (p + 1 + s) % nj).wait_recv())
        rows = lax.broadcasted_iota(jnp.int32, (rank, rank), 0)
        lanes = lax.broadcasted_iota(jnp.int32, (rank, rank), 1)
        value = gram_c[...] * g3[t].reshape(rank, rank)
        system[...] = value + jnp.where(rows == lanes, RIDGE, 0.0)
        sweep(system)

    gram_local(0, b_ref[...])
    pl.semaphore_wait(barrier, nj - 1 + nz - 1)

    def a_copy(to, slot):
        return send(b_ref, b_all.at[slot], a_s.at[to], a_r.at[slot], (to, p))

    gram_1(0)
    each(nz - 1, lambda s: a_copy((z + 1 + s) % nz, z).start())
    b_all[z] = b_ref[...]

    c_pad[...] = jnp.zeros_like(c_pad)
    c_pad[0:layers, :] = c_ref[...]
    gram_c[...] = cross(c_pad[0:16, :], c_pad[0:16, :])
    c_turn[...] = c_pad[...].T

    strip = min(256, high)
    for k in range(layers):
        t_copies[k].wait()

        def convert(s, k=k):
            at = pl.multiple_of(s * strip, strip)
            hi, lo = split2(t_f32[k, pl.ds(at, strip), :])
            t_hi[pl.ds(at, strip), k * wide : (k + 1) * wide] = hi
            t_lo[pl.ds(at, strip), k * wide : (k + 1) * wide] = lo

        each(high // strip, convert)

    gram_2(0)

    each(nz - 1, lambda s: a_copy(z, (z + 1 + s) % nz).wait_recv())
    rows_b = b_all[...].reshape(wide, rank)
    for k in range(layers):
        hi, lo = split2(rows_b * c_ref[k : k + 1, :])
        w_hi[k * wide : (k + 1) * wide, :] = hi
        w_lo[k * wide : (k + 1) * wide, :] = lo

    group = nq // CHUNKS

    def c1_copy(chip):
        return send(tot.at[chip, 1 - c], sib.at[chip], c1_s.at[chip], c1_r.at[chip], (z, other))

    def c2_copy(to, slot):
        return send(comb.at[to], landed.at[slot], c2_s.at[to], c2_r.at[slot], (z, 2 * to + c))

    def chunk_of(s):
        return (q // group + 1 + s) % CHUNKS

    def multiply(s):
        x = chunk_of(s)
        size = high // CHUNKS
        at = pl.multiple_of(x * size, size)
        th, tl = t_hi[pl.ds(at, size), :], t_lo[pl.ds(at, size), :]
        total = dot(th, w_hi[...]) + dot(tl, w_hi[...]) + dot(th, w_lo[...])
        tot[pl.ds(x * group, group)] = total.reshape(group, 2, per, rank)
        each(group, lambda i: c1_copy(x * group + i).start())

    def merge(s):
        x = chunk_of(s)

        def one(i):
            chip = x * group + i
            c1_copy(chip).wait_recv()
            value = tot[chip, c] + sib[chip]

            @pl.when(chip != q)
            def _():
                comb[chip] = value
                c2_copy(chip, q).start()

            @pl.when(chip == q)
            def _():
                landed[q] = value

        each(group, one)

    multiply(0)
    gram_3(0)

    def go(s):
        multiply(s + 1)
        merge(s)

    each(CHUNKS - 1, go)
    merge(CHUNKS - 1)

    gram_4(0)

    each(nq - 1, lambda s: c2_copy(q, (q + 1 + s) % nq).wait_recv())
    moments = landed[0]
    for s in range(1, nq):
        moments = moments + landed[s]
    rows_a = -full_dot(moments, system[...])
    fa_ref[...] = rows_a
    a_all[p] = rows_a

    def e1_copy(to, slot):
        return send(fa_ref, a_all.at[slot], e1_s.at[to], e_r.at[slot], (z, to))

    def e2_copy(slot):
        return send(a_all.at[slot], a_all.at[slot], e2_s.at[slot], e_r.at[slot], (z, other))

    gram_local(1, rows_a)
    gram_1(1)
    e1_copy(other, p).start()
    each(nq - 1, lambda s: e1_copy(2 * ((q + 1 + s) % nq) + c, p).start())
    gram_2(1)

    def forward(s):
        slot = 2 * ((q + nq - 1 - s) % nq) + c
        e1_copy(p, slot).wait_recv()
        e2_copy(slot).start()

    each(nq - 1, forward)
    gram_3(1)
    each(nq, lambda s: e2_copy(2 * ((q + nq - s) % nq) + 1 - c).wait_recv())

    piece = min(256, high)

    def turn(s):
        at = pl.multiple_of(s * piece, piece)
        block = a_all[pl.ds(s * (piece // per), piece // per)].reshape(piece, rank)
        hi, lo = split2(block.T)
        at_hi[:, pl.ds(at, piece)] = hi
        at_lo[:, pl.ds(at, piece)] = lo

    each(high // piece, turn)

    total_b = jnp.zeros((rank, wide), F32)
    for k in range(layers):
        th, tl = t_hi[:, k * wide : (k + 1) * wide], t_lo[:, k * wide : (k + 1) * wide]
        value = dot(at_hi[...], th) + dot(at_lo[...], th) + dot(at_hi[...], tl)
        total_b = total_b + value * c_turn[:, k : k + 1]
    tot_b[...] = total_b.T.reshape(nz, per, rank)

    def h_copy(to, slot):
        return send(tot_b.at[to], h_land.at[slot], h_s.at[to], h_r.at[slot], (to, p))

    each(nz - 1, lambda s: h_copy((z + 1 + s) % nz, z).start())
    h_land[z] = tot_b[z]

    gram_4(1)

    each(nz - 1, lambda s: h_copy(z, (z + 1 + s) % nz).wait_recv())
    moments = h_land[0]
    for s in range(1, nz):
        moments = moments + h_land[s]
    fb_ref[...] = -full_dot(moments, system[...])

    each(nz - 1, lambda s: a_copy((z + 1 + s) % nz, z).wait_send())
    each(nz - 1, lambda s: h_copy((z + 1 + s) % nz, z).wait_send())
    for t in range(2):
        each(nj - 1, lambda s: g1_copy(t, (p + 1 + s) % nj, p).wait_send())
        each(nz - 1, lambda s: g2_copy(t, (z + 1 + s) % nz, z).wait_send())
        each(nj - 1, lambda s: g3_copy(t, (p + 1 + s) % nj, p).wait_send())
    each(nq, lambda s: c1_copy(s).wait_send())
    each(nq - 1, lambda s: c2_copy((q + 1 + s) % nq, q).wait_send())
    e1_copy(other, p).wait_send()
    each(nq - 1, lambda s: e1_copy(2 * ((q + 1 + s) % nq) + c, p).wait_send())
    each(nq - 1, lambda s: e2_copy(2 * ((q + nq - 1 - s) % nq) + c).wait_send())


def solution(mesh):
    nz, nj = mesh.shape["ia"], mesh.shape["ja"]
    nq = nj // 2

    def local(tensor, factor_b, factor_c):
        layers, high, wide = tensor.shape
        per, rank = factor_b.shape
        slab = rank // nj
        vm = pltpu.VMEM
        sem = lambda *shape: pltpu.SemaphoreType.DMA(shape)
        out = jax.ShapeDtypeStruct((per, rank), F32)
        whole = pl.BlockSpec(memory_space=pltpu.VMEM)
        return pl.pallas_call(
            functools.partial(kernel, nz, nj),
            out_shape=(out, out),
            in_specs=[pl.BlockSpec(memory_space=pl.ANY), whole, whole],
            out_specs=(whole, whole),
            scratch_shapes=[
                vm((layers, high, wide), F32),
                vm((high, layers * wide), BF16), vm((high, layers * wide), BF16),
                vm((layers * wide, rank), BF16), vm((layers * wide, rank), BF16),
                vm((nz, per, rank), F32),
                vm((128, rank), F32), vm((rank, 128), F32), vm((rank, rank), F32),
                vm((2, nj, slab, rank), F32), vm((2, nj, slab, rank), F32), vm((2, slab, rank), F32),
                vm((2, nz, slab, rank), F32), vm((2, slab, rank), F32), vm((2, nj, slab, rank), F32),
                vm((rank, rank), F32),
                vm((nq, 2, per, rank), F32), vm((nq, per, rank), F32), vm((nq, per, rank), F32),
                vm((nq, per, rank), F32), vm((nj, per, rank), F32),
                vm((rank, high), BF16), vm((rank, high), BF16),
                vm((nz, per, rank), F32), vm((nz, per, rank), F32),
                sem(layers), sem(nz), sem(nz), sem(2, nj), sem(2, nj), sem(2, nz), sem(2, nz), sem(2, nj), sem(2, nj),
                sem(nq), sem(nq), sem(nq), sem(nq), sem(nj), sem(nj), sem(nj), sem(nz), sem(nz),
            ],
            compiler_params=pltpu.CompilerParams(
                collective_id=0, has_side_effects=True, vmem_limit_bytes=48 * 1024 * 1024
            ),
            cost_estimate=pl.CostEstimate(
                flops=4 * layers * high * wide * rank, bytes_accessed=4 * layers * high * wide, transcendentals=0
            ),
        )(tensor, factor_b, factor_c)

    in_specs = (P(None, "ia", "ja"), P(("ja", "ia"), None), P())
    out_specs = (P(("ia", "ja"), None), P(("ja", "ia"), None))
    return jax.shard_map(local, mesh=mesh, in_specs=in_specs, out_specs=out_specs, check_vma=False)
```

time: 691 us -> 79.1 us (0.11); the launches traced: 683 us -> 78.9 us
  waiting for transfers between devices: 481 us -> 0 us
  other arithmetic: 110 us -> 0 us
  Pallas kernels: 0 us -> 75.6 us
  matrix products: 35.7 us -> 0 us
  blocking collectives: 23.5 us -> 0 us
  between operations: 18.3 us -> 0.65 us
  local copies, waits for them, and re-layouts: 13.7 us -> 2.68 us
    psum x2 -> x0, waiting for transfers between devices: 471 us -> none  [the longest x1 249 us: local(): gram_a = lax.psum(cross(factor_a, factor_a), ('ia', 'ja'))]
    another operation x20 -> x0, other arithmetic: 109 us -> none  [the longest x13 68.7 us: solve_rows(): lower = jnp.linalg.cholesky(system)]
    pallas_call x0 -> x1, Pallas kernels: none -> 75.6 us  [local(): pl.pallas_call(functools.partial(kernel, nz, nj), out_shape=(out, out), i...]
    dot_general x5 -> x0, matrix products: 31 us -> none  [the longest x1 16.6 us: local(): jnp.einsum('knj,knr->jr', slab, weighted, precision=highest, preferred_el...]
    all_gather x1 -> x0, blocking collectives: 23.5 us -> none  [local(): lax.all_gather(factor_b, 'ia', axis=0, tiled=True)[None, :, :]]
    another operation x21 -> x0, local copies, waits for them, and re-layouts: 9.44 us -> none  [the longest x17 9.39 us: solve_rows(): lax.linalg.triangular_solve(lower, moments, left_side=False, lower=True,...]
    unnamed x7 -> x0, waiting for transfers between devices: 9.23 us -> none
  transfers between devices with their start and end apart: 5 -> 0, of which waited for: 3 -> 0; matrix products, arithmetic and copies ran while one was open for 19% -> 0% of each run, Pallas kernels for 0% -> 0%
where the time goes in v1:
time: 79.1 us; the launch traced here: 78.9 us
  Pallas kernels  75.6 us (96%)
  local copies, waits for them, and re-layouts  2.68 us (3%)
    pallas_call x1, Pallas kernels, local(): pl.pallas_call(functools.partial(kernel, nz, nj), out_shape=(out, out), i...  75.6 us
    unnamed x6, local copies, waits for them, and re-layouts  2.68 us

profile of v1, /device:TPU:1, one launch (start us, length us, event | category | flops | bytes accessed | tf_op | source)
XLA Modules:
  0.0 78.9 jit_solution(15211638128970063141)
XLA Ops:
  0.6 0.0 copy-start
  0.6 0.7 copy-done
  1.4 0.0 copy-start.1
  1.4 0.7 copy-done.1
  2.1 75.6 %shard_map.50 = (f32[32,256]{1,0:T(8,128)S(1)}, f32[32,256]{1,0:T(8,128)S(1)}) custom-call(f32[8,1024,256]{2,1,0:T(8,128)} %t_hbm.1, f32[32,256]{1,0:T(8,128)S(1)} %copy-done, f32[8,256]{1,0:T(8,128)S(1)} %copy-done.1), custom_call_target="tpu_custom_call" | custom-call | flops 2147483648 | bytes 8388608 | tf_op jit(solution)/shard_map/pallas_call | solution.py:360
  77.7 0.6 copy.7
  78.3 0.6 copy.8
Async XLA Ops:
  0.6 0.8 copy-start
  1.4 0.7 copy-start.1

commit v2 on v1

v2 whole, which is shorter than its diff:
```python
import functools

import jax
import jax.numpy as jnp
from jax import lax
from jax.experimental import pallas as pl
from jax.experimental.pallas import tpu as pltpu
from jax.sharding import PartitionSpec as P

RIDGE = 0.001
MESH = pl.DeviceIdType.MESH
F32 = jnp.float32
BF16 = jnp.bfloat16
PB = 16
CHUNKS = 4
EARLY = 4


def split2(x):
    high = x.astype(BF16)
    return high, (x - high.astype(F32)).astype(BF16)


def split3(x):
    high = x.astype(BF16)
    rest = x - high.astype(F32)
    mid = rest.astype(BF16)
    return high, mid, (rest - mid.astype(F32)).astype(BF16)


def cross(left, right):
    lh, lm, ll = split3(left)
    rh, rm, rl = split3(right)
    a = jnp.concatenate([lh, lh, lm, lh, lm, ll], axis=0)
    b = jnp.concatenate([rh, rm, rh, rl, rm, rh], axis=0)
    return lax.dot_general(a, b, (((0,), (0,)), ((), ())), preferred_element_type=F32)


def row_of(block, at):
    return jnp.broadcast_to(block[at : at + 1, :], block.shape)


def eliminate(cols, panel, width):
    row = lax.broadcasted_iota(jnp.int32, (8, width), 0)
    halves = range(PB // 8)
    for j in range(0, PB, 2):
        h, jj = j // 8, j % 8
        u0, u1 = cols[j], cols[j + 1]
        first, second = row == jj, row == jj + 1
        pair = first | second
        a, b, d = row_of(u0[h], jj), row_of(u0[h], jj + 1), row_of(u1[h], jj + 1)
        scale = 1.0 / (a * d - b * b)
        w0 = [d * u0[g] - b * u1[g] for g in halves]
        w1 = [a * u1[g] - b * u0[g] for g in halves]
        w0[h] = jnp.where(first, -d, jnp.where(second, b, w0[h]))
        w1[h] = jnp.where(first, b, jnp.where(second, -a, w1[h]))

        def step(target):
            q0, q1 = row_of(target[h], jj), row_of(target[h], jj + 1)
            base = [jnp.where(pair, 0.0, target[g]) if g == h else target[g] for g in halves]
            return [base[g] - scale * (w0[g] * q0 + w1[g] * q1) for g in halves]

        cols = [step(col) if l > j + 1 else None for l, col in enumerate(cols)]
        panel = [step(part) for part in panel]
    return panel


def columns_of(panel, at, width):
    lanes = lax.broadcasted_iota(jnp.int32, panel.shape, 1)
    cols = []
    for l in range(PB):
        col = jnp.sum(jnp.where(lanes == at + l, panel, 0.0), axis=1, keepdims=True)
        col = jnp.broadcast_to(col, (PB, width))
        cols.append([col[8 * g : 8 * g + 8] for g in range(PB // 8)])
    return cols


def sweep(s_ref, between=()):
    size = s_ref.shape[0]
    steps = size // PB
    lanes = lax.broadcasted_iota(jnp.int32, (PB, size), 1)
    rows = lax.broadcasted_iota(jnp.int32, (PB, size), 0)
    whole = lax.broadcasted_iota(jnp.int32, (size, size), 1)
    width = 128

    def update(at, source, fresh):
        kept = jnp.where((whole >= at) & (whole < at + PB), 0.0, s_ref[...])
        s_ref[...] = kept - cross(source, fresh)

    def step(k, carry):
        panel, before, done = carry
        at = pl.multiple_of(k * PB, PB)
        after = pl.multiple_of(((k + 1) % steps) * PB, PB)
        cols = columns_of(panel, at, width)
        inside = (lanes >= at) & (lanes < at + PB)
        source = jnp.where(inside, jnp.where(lanes == at + rows, -1.0, 0.0), panel)
        parts = [
            [source[8 * g : 8 * g + 8, w * width : (w + 1) * width] for g in range(PB // 8)]
            for w in range(size // width)
        ]
        update(at - PB, before, done)
        following = s_ref[pl.ds(after, PB), :]
        factors = columns_of(following, at, width)
        parts = eliminate(cols, parts, width)
        fresh = jnp.concatenate([jnp.concatenate(part, axis=0) for part in parts], axis=1)
        s_ref[pl.ds(at, PB), :] = jnp.zeros((PB, size), F32)
        following = jnp.where(inside, 0.0, following)
        parts = [
            [following[8 * g : 8 * g + 8, w * width : (w + 1) * width] for g in range(PB // 8)]
            for w in range(size // width)
        ]
        for w in range(size // width):
            for l in range(PB):
                line = jnp.broadcast_to(fresh[l : l + 1, w * width : (w + 1) * width], (8, width))
                for g in range(PB // 8):
                    parts[w][g] = parts[w][g] - factors[l][g] * line
        following = jnp.concatenate([jnp.concatenate(part, axis=0) for part in parts], axis=1)
        return following, source, fresh

    blank = jnp.zeros((PB, size), F32)
    carry = (s_ref[0:PB, :], blank, blank)
    start = 0
    for end, action in between:
        carry = lax.fori_loop(start, end, step, carry)
        action()
        start = end
    _, before, done = lax.fori_loop(start, steps, step, carry)
    update(size - PB, before, done)


def dot(a, b):
    return jnp.dot(a, b, preferred_element_type=F32)


def full_dot(a, b):
    return jnp.dot(a, b, precision=lax.Precision.HIGHEST, preferred_element_type=F32)


def kernel(nz, nj, t_hbm, b_hbm, c_hbm, fa_ref, fb_ref,
           t_f32, t_hi, t_lo, w_hi, w_lo, b_all, b_sib, c_v, c_pad, c_turn, gram_c,
           gram, g1, g1_sum, g2, g2_sum, g3, inverse, system,
           tot, sib, comb, landed, own, m_all, total_b, tot_b, h_land,
           t_sem, in_sem, a_s, a_r, s_s, s_r, g1_s, g1_r, g2_s, g2_r, g3_s, g3_r, g4_s, g4_r,
           c1_s, c1_r, c2_s, c2_r, e1_s, e1_r, e2_s, e2_r, h_s, h_r):
    z, p = lax.axis_index("ia"), lax.axis_index("ja")
    q, c = p // 2, p % 2
    nq = nj // 2
    per, rank = own.shape
    layers, high, wide = t_hbm.shape
    half = rank // 2
    other = p + 1 - 2 * c

    def send(src, dst, s_sem, r_sem, to):
        return pltpu.make_async_remote_copy(
            src_ref=src, dst_ref=dst, send_sem=s_sem, recv_sem=r_sem, device_id=to, device_id_type=MESH
        )

    def arrived(ref, sem):
        pltpu.make_async_copy(ref, ref, sem).wait()

    def each(n, body):
        lax.fori_loop(0, n, lambda s, carry: (body(s), carry)[1], 0)

    def round_z(body):
        each(nz - 1, lambda s: body((z + 1 + (s + nz // 2 - 1) % (nz - 1)) % nz))

    def round_half(n, body):
        each(nz // 2 - 1, lambda s: body(n * (nz // 2) + (z + 1 + s) % (nz // 2)))

    def round_q(body):
        far = (nq // 2 + nq // 8 - 1) % (nq - 1)
        each(nq - 1, lambda s: body((q + 1 + (s + far) % (nq - 1)) % nq))

    barrier = pltpu.get_barrier_semaphore()
    round_q(lambda to: pl.semaphore_signal(barrier, inc=1, device_id=(z, 2 * to + c), device_id_type=MESH))
    round_z(lambda to: pl.semaphore_signal(barrier, inc=1, device_id=(to, p), device_id_type=MESH))
    pl.semaphore_signal(barrier, inc=1, device_id=(z, other), device_id_type=MESH)

    b_copy = pltpu.make_async_copy(b_hbm, b_all.at[z], in_sem.at[0])
    c_copy = pltpu.make_async_copy(c_hbm, c_v, in_sem.at[1])
    b_copy.start()
    c_copy.start()
    t_copies = [pltpu.make_async_copy(t_hbm.at[k], t_f32.at[k], t_sem.at[k]) for k in range(layers)]
    for copy in t_copies:
        copy.start()

    def g1_copy(t, to, slot):
        return send(gram.at[t, to], g1.at[t, slot], g1_s.at[t], g1_r.at[t], (z, 2 * to + c))

    def g2_copy(t, to, slot):
        return send(g1_sum.at[t], g2.at[t, slot], g2_s.at[t], g2_r.at[t], (to, p))

    def g3_copy(t, to, slot):
        return send(g2_sum.at[t], g3.at[t, c, slot], g3_s.at[t], g3_r.at[t], (z, 2 * to + c))

    def g4_copy(t, side):
        return send(g3.at[t, side], g3.at[t, side], g4_s.at[t], g4_r.at[t], (z, other))

    def gram_1(t, mine, twin):
        at = pl.multiple_of(c * half, half)
        left = jnp.concatenate([mine[:, pl.ds(at, half)], twin[:, pl.ds(at, half)]], axis=0)
        right = jnp.concatenate([mine[...], twin[...]], axis=0)
        value = cross(left, right).reshape(nq, half // nq, rank)
        gram[t] = value
        round_q(lambda to: g1_copy(t, to, q).start())
        g1[t, q] = gram[t, q]

    def gram_2(t):
        arrived(g1.at[t, pl.ds(0, nq - 1)], g1_r.at[t])
        total = g1[t, 0]
        for s in range(1, nq):
            total = total + g1[t, s]
        g1_sum[t] = total
        round_z(lambda to: g2_copy(t, to, z).start())
        g2[t, z] = total

    def gram_3(t):
        arrived(g2.at[t, pl.ds(0, nz - 1)], g2_r.at[t])
        total = g2[t, 0]
        for s in range(1, nz):
            total = total + g2[t, s]
        g2_sum[t] = total
        round_q(lambda to: g3_copy(t, to, q).start())
        g3[t, c, q] = total

    def gram_4(t):
        arrived(g3.at[t, 0, pl.ds(0, nq - 1)], g3_r.at[t])
        g4_copy(t, c).start()

    def gram_5(t):
        g4_copy(t, 1 - c).wait_recv()
        return g3[t].reshape(rank, rank)

    def system_of(value):
        rows = lax.broadcasted_iota(jnp.int32, (rank, rank), 0)
        lanes = lax.broadcasted_iota(jnp.int32, (rank, rank), 1)
        return gram_c[...] * value + jnp.where(rows == lanes, RIDGE, 0.0)

    def s_copy():
        return send(b_all.at[z], b_sib, s_s.at[0], s_r.at[0], (z, other))

    def a_copy(to, slot, which):
        return send(b_all.at[z], b_all.at[slot], a_s.at[0], a_r.at[which], (to, p))

    b_copy.wait()
    c_copy.wait()
    pl.semaphore_wait(barrier, nq - 1 + nz - 1 + 1)
    s_copy().start()
    round_half(z // (nz // 2), lambda to: a_copy(to, z, 0).start())
    each(nz // 2, lambda s: a_copy((1 - z // (nz // 2)) * (nz // 2) + (z + s) % (nz // 2), z, 1).start())
    s_copy().wait_recv()
    gram_1(0, b_all.at[z], b_sib)

    c_pad[...] = jnp.zeros_like(c_pad)
    c_pad[0:layers, :] = c_v[...]
    gram_c[...] = cross(c_pad[0:16, :], c_pad[0:16, :])
    c_turn[...] = c_pad[...].T

    hw = wide // 2
    sw = layers * hw
    strip = min(256, high)
    for k in range(layers):
        t_copies[k].wait()

        def convert(s, k=k):
            at = pl.multiple_of(s * strip, strip)
            hi, lo = split2(t_f32[k, pl.ds(at, strip), :])
            for n in range(2):
                to = n * sw + k * hw
                t_hi[pl.ds(at, strip), to : to + hw] = hi[:, n * hw : (n + 1) * hw]
                t_lo[pl.ds(at, strip), to : to + hw] = lo[:, n * hw : (n + 1) * hw]

        each(high // strip, convert)

    near = z // (nz // 2)

    def weights(n):
        block = b_all[pl.ds(n * (nz // 2), nz // 2)].reshape(hw, rank)
        for k in range(layers):
            hi, lo = split2(block * c_v[k : k + 1, :])
            at = pl.multiple_of(n * sw + k * hw, hw)
            w_hi[pl.ds(at, hw), :] = hi
            w_lo[pl.ds(at, hw), :] = lo

    def product(n, x):
        size = high // CHUNKS
        at, to = pl.multiple_of(x * size, size), pl.multiple_of(n * sw, sw)
        th, tl = t_hi[pl.ds(at, size), pl.ds(to, sw)], t_lo[pl.ds(at, size), pl.ds(to, sw)]
        wh, wl = w_hi[pl.ds(to, sw), :], w_lo[pl.ds(to, sw), :]
        return (dot(th, wh) + dot(tl, wh) + dot(th, wl)).reshape(nq // CHUNKS, 2, per, rank)

    if nz // 2 > 1:
        arrived(b_all.at[pl.ds(0, nz // 2 - 1)], a_r.at[0])
    weights(near)

    def first(x):
        tot[pl.ds(x * (nq // CHUNKS), nq // CHUNKS)] = product(near, x)

    each(CHUNKS, first)
    gram_2(0)
    arrived(b_all.at[pl.ds(0, nz // 2)], a_r.at[1])
    weights(1 - near)

    group = nq // CHUNKS

    def c1_copy(chip):
        return send(tot.at[chip, 1 - c], sib.at[chip], c1_s.at[0], c1_r.at[chip // group], (z, other))

    def c2_copy(to, slot):
        return send(comb.at[to], landed.at[slot], c2_s.at[0], c2_r.at[0], (z, 2 * to + c))

    def chunk_of(s):
        return (q // group + 1 + s) % CHUNKS

    def multiply(s):
        x = chunk_of(s)
        tot[pl.ds(x * group, group)] += product(1 - near, x)
        each(group, lambda i: c1_copy(x * group + i).start())

    def merge(s):
        x = chunk_of(s)

        arrived(sib.at[pl.ds(0, group)], c1_r.at[x])

        def one(i):
            chip = x * group + i
            value = tot[chip, c] + sib[chip]

            @pl.when(chip != q)
            def _():
                comb[chip] = value
                c2_copy(chip, q).start()

            @pl.when(chip == q)
            def _():
                landed[q] = value

        each(group, one)

    multiply(0)

    def go(s):
        multiply(s + 1)
        merge(s)

    each(CHUNKS - 1, go)
    merge(CHUNKS - 1)
    gram_3(0)

    def e1_copy(to):
        return send(own, m_all.at[p], e1_s.at[0], e1_r.at[q // group], (z, to))

    def twin_copy():
        return send(own, m_all.at[p], e1_s.at[1], e1_r.at[CHUNKS], (z, other))

    def e2_copy(slot, x):
        return send(m_all.at[slot], m_all.at[slot], e2_s.at[0], e2_r.at[x], (z, other))

    def moments_a():
        arrived(landed.at[pl.ds(0, nq - 1)], c2_r.at[0])
        moments = landed[0]
        for s in range(1, nq):
            moments = moments + landed[s]
        own[...] = moments
        twin_copy().start()
        m_all[p] = moments

    def share_moments():
        twin_copy().wait_recv()
        gram_1(1, own, m_all.at[other])
        round_q(lambda to: e1_copy(2 * to + c).start())

    gram_4(0)
    inverse[...] = system_of(gram_5(0))
    sweep(inverse, ((EARLY, moments_a), (EARLY + 2, share_moments)))
    fa_ref[...] = -full_dot(own[...], inverse[...])

    def group_of(s):
        return (q // group + s + s // 2 - 2 * (s // 3)) % CHUNKS

    def landing(s, sem):
        @pl.when(s == 0)
        def _():
            if group > 1:
                arrived(m_all.at[pl.ds(0, group - 1)], sem)

        @pl.when(s != 0)
        def _():
            arrived(m_all.at[pl.ds(0, group)], sem)

    def forward(s):
        x = group_of(s)
        landing(s, e1_r.at[x])

        def one(i):
            chip = x * group + i

            @pl.when(chip != q)
            def _():
                e2_copy(2 * chip + c, x).start()

        each(group, one)

    def back(s):
        x = group_of(s)
        landing(s, e2_r.at[x])
        size = high // CHUNKS
        at = pl.multiple_of(x * size, size)
        block = m_all[pl.ds(x * 2 * group, 2 * group)].reshape(size, rank)
        ah, al = split2(-full_dot(block, inverse[...]).T)
        for n in range(2):
            part = total_b[n]
            for m in range(layers // 2):
                to = n * sw + m * wide
                th, tl = t_hi[pl.ds(at, size), to : to + wide], t_lo[pl.ds(at, size), to : to + wide]
                value = dot(ah, th) + dot(al, th) + dot(ah, tl)
                part = part + value[:, 0:hw] * c_turn[:, 2 * m : 2 * m + 1]
                part = part + value[:, hw:wide] * c_turn[:, 2 * m + 1 : 2 * m + 2]
            total_b[n] = part

    total_b[...] = jnp.zeros_like(total_b)
    forward(0)
    gram_2(1)

    def go_back(s):
        forward(s + 1)
        back(s)

        @pl.when(s == 1)
        def _():
            gram_3(1)

    each(CHUNKS - 1, go_back)
    back(CHUNKS - 1)

    for n in range(2):
        tot_b[n * (nz // 2) : (n + 1) * (nz // 2)] = total_b[n].T.reshape(nz // 2, per, rank)

    def h_copy(to, slot):
        return send(tot_b.at[to], h_land.at[slot], h_s.at[0], h_r.at[0], (to, p))

    round_z(lambda to: h_copy(to, z).start())
    gram_4(1)
    h_land[z] = tot_b[z]

    system[...] = full_dot(inverse[...], gram_5(1))
    system[...] = system_of(full_dot(system[...], inverse[...]))
    sweep(system)

    arrived(h_land.at[pl.ds(0, nz - 1)], h_r.at[0])
    moments = h_land[0]
    for s in range(1, nz):
        moments = moments + h_land[s]
    fb_ref[...] = -full_dot(moments, system[...])

    s_copy().wait_send()
    arrived(b_all.at[pl.ds(0, nz - 1)], a_s.at[0])
    arrived(h_land.at[pl.ds(0, nz - 1)], h_s.at[0])
    for t in range(2):
        arrived(g1.at[t, pl.ds(0, nq - 1)], g1_s.at[t])
        arrived(g2.at[t, pl.ds(0, nz - 1)], g2_s.at[t])
        arrived(g3.at[t, 0, pl.ds(0, nq - 1)], g3_s.at[t])
        g4_copy(t, c).wait_send()
    arrived(sib, c1_s.at[0])
    arrived(landed.at[pl.ds(0, nq - 1)], c2_s.at[0])
    arrived(m_all.at[pl.ds(0, nq - 1)], e1_s.at[0])
    twin_copy().wait_send()
    arrived(m_all.at[pl.ds(0, nq - 1)], e2_s.at[0])


def solution(mesh):
    nz, nj = mesh.shape["ia"], mesh.shape["ja"]
    nq = nj // 2

    def local(tensor, factor_b, factor_c):
        layers, high, wide = tensor.shape
        per, rank = factor_b.shape
        slab = rank // nj
        vm = pltpu.VMEM
        sem = lambda *shape: pltpu.SemaphoreType.DMA(shape)
        out = jax.ShapeDtypeStruct((per, rank), F32)
        whole = pl.BlockSpec(memory_space=pltpu.VMEM)
        anywhere = pl.BlockSpec(memory_space=pltpu.HBM)
        return pl.pallas_call(
            functools.partial(kernel, nz, nj),
            out_shape=(out, out),
            in_specs=[anywhere] * 3,
            out_specs=(whole, whole),
            scratch_shapes=[
                vm((layers, high, wide), F32),
                vm((high, layers * wide), BF16), vm((high, layers * wide), BF16),
                vm((layers * wide, rank), BF16), vm((layers * wide, rank), BF16),
                vm((nz, per, rank), F32), vm((per, rank), F32), vm((layers, rank), F32),
                vm((128, rank), F32), vm((rank, 128), F32), vm((rank, rank), F32),
                vm((2, nq, slab, rank), F32), vm((2, nq, slab, rank), F32), vm((2, slab, rank), F32),
                vm((2, nz, slab, rank), F32), vm((2, slab, rank), F32), vm((2, 2, nq, slab, rank), F32),
                vm((rank, rank), F32), vm((rank, rank), F32),
                vm((nq, 2, per, rank), F32), vm((nq, per, rank), F32), vm((nq, per, rank), F32),
                vm((nq, per, rank), F32), vm((per, rank), F32), vm((nj, per, rank), F32),
                vm((2, rank, wide // 2), F32),
                vm((nz, per, rank), F32), vm((nz, per, rank), F32),
                sem(layers), sem(2), sem(1), sem(2), sem(1), sem(1),
                sem(2), sem(2), sem(2), sem(2), sem(2), sem(2), sem(2), sem(2),
                sem(1), sem(CHUNKS), sem(1), sem(1), sem(2), sem(CHUNKS + 1), sem(1), sem(CHUNKS), sem(1), sem(1),
            ],
            compiler_params=pltpu.CompilerParams(
                collective_id=0, has_side_effects=True, vmem_limit_bytes=48 * 1024 * 1024
            ),
            cost_estimate=pl.CostEstimate(
                flops=4 * layers * high * wide * rank, bytes_accessed=4 * layers * high * wide, transcendentals=0
            ),
        )(tensor, factor_b, factor_c)

    in_specs = (P(None, "ia", "ja"), P(("ja", "ia"), None), P())
    out_specs = (P(("ia", "ja"), None), P(("ja", "ia"), None))
    return jax.shard_map(local, mesh=mesh, in_specs=in_specs, out_specs=out_specs, check_vma=False)
```

time: 79.1 us -> 70.2 us (0.89)
  Pallas kernels: 75.6 us -> 66.7 us
    pallas_call x1, Pallas kernels: 75.6 us -> 66.7 us  [local(): pl.pallas_call(functools.partial(kernel, nz, nj), out_shape=(out, out), i...]
where the time goes in v2:
time: 70.2 us; the launch traced here: 70 us
  Pallas kernels  66.7 us (95%)
  local copies, waits for them, and re-layouts  2.68 us (4%)
    pallas_call x1, Pallas kernels, local(): pl.pallas_call(functools.partial(kernel, nz, nj), out_shape=(out, out), i...  66.7 us
    unnamed x6, local copies, waits for them, and re-layouts  2.68 us

profile of v2, /device:TPU:1, one launch (start us, length us, event | category | flops | bytes accessed | tf_op | source)
XLA Modules:
  0.0 70.0 jit_solution(16926804664657972293)
XLA Ops:
  0.6 0.0 copy-start
  0.6 0.7 %copy-done = f32[32,256]{1,0:T(8,128)S(1)} copy-done((f32[32,256]{1,0:T(8,128)S(1)}, f32[32,256]{1,0:T(8,128)}, u32[]{:S(2)}) %copy-start) | copy-done | bytes 32792
  1.4 0.0 copy-start.1
  1.4 0.7 copy-done.1
  2.1 66.7 %shard_map.50 = (f32[32,256]{1,0:T(8,128)S(1)}, f32[32,256]{1,0:T(8,128)S(1)}) custom-call(f32[8,1024,256]{2,1,0:T(8,128)} %t_hbm.1, f32[32,256]{1,0:T(8,128)S(1)} %copy-done, f32[8,256]{1,0:T(8,128)S(1)} %copy-done.1), custom_call_target="tpu_custom_call" | custom-call | flops 2147483648 | bytes 8388608 | tf_op jit(solution)/shard_map/pallas_call | solution.py:484
  68.8 0.6 copy.7
  69.4 0.6 copy.8
Async XLA Ops:
  0.6 0.8 %copy-start = (f32[32,256]{1,0:T(8,128)S(1)}, f32[32,256]{1,0:T(8,128)}, u32[]{:S(2)}) copy-start(f32[32,256]{1,0:T(8,128)} %b_hbm.1) | copy-start | bytes 98308
  1.4 0.7 copy-start.1

commit v3 on v2

--- a/solution.py
+++ b/solution.py
@@ -13,7 +13,7 @@
 BF16 = jnp.bfloat16
 PB = 16
 CHUNKS = 4
-EARLY = 4
+MIDDLE = 5
 
 
 def split2(x):
@@ -75,57 +75,64 @@
     return cols
 
 
+def parts_of(panel, width):
+    return [
+        [panel[8 * g : 8 * g + 8, w * width : (w + 1) * width] for g in range(PB // 8)]
+        for w in range(panel.shape[1] // width)
+    ]
+
+
+def whole_of(parts):
+    return jnp.concatenate([jnp.concatenate(part, axis=0) for part in parts], axis=1)
+
+
+def less(panel, factors, fresh, width):
+    parts = parts_of(panel, width)
+    for l in range(PB):
+        for w, part in enumerate(parts):
+            line = jnp.broadcast_to(fresh[l : l + 1, w * width : (w + 1) * width], (8, width))
+            for g in range(PB // 8):
+                part[g] = part[g] - factors[l][g] * line
+    return whole_of(parts)
+
+
 def sweep(s_ref, between=()):
     size = s_ref.shape[0]
-    steps = size // PB
+    steps = size // (2 * PB)
     lanes = lax.broadcasted_iota(jnp.int32, (PB, size), 1)
     rows = lax.broadcasted_iota(jnp.int32, (PB, size), 0)
     whole = lax.broadcasted_iota(jnp.int32, (size, size), 1)
     width = 128
 
-    def update(at, source, fresh):
-        kept = jnp.where((whole >= at) & (whole < at + PB), 0.0, s_ref[...])
+    def step(k, carry):
+        at = pl.multiple_of(k * 2 * PB, 2 * PB)
+        mid = at + PB
+        upper, lower = s_ref[pl.ds(at, PB), :], s_ref[pl.ds(pl.multiple_of(mid, PB), PB), :]
+        in_upper, in_lower = (lanes >= at) & (lanes < mid), (lanes >= mid) & (lanes < mid + PB)
+        minus_upper = jnp.where(lanes == at + rows, -1.0, 0.0)
+        minus_lower = jnp.where(lanes == mid + rows, -1.0, 0.0)
+        cols = columns_of(upper, at, width)
+        factors = columns_of(lower, at, width)
+        first = whole_of(eliminate(cols, parts_of(jnp.where(in_upper, minus_upper, upper), width), width))
+        backs = columns_of(first, mid, width)
+        rest = less(jnp.where(in_upper, 0.0, lower), factors, first, width)
+        cols = columns_of(rest, mid, width)
+        second = whole_of(eliminate(cols, parts_of(jnp.where(in_lower, minus_lower, rest), width), width))
+        first = less(jnp.where(in_lower, 0.0, first), backs, second, width)
+        fresh = jnp.concatenate([first, second], axis=0)
+        both = in_upper | in_lower
+        source = jnp.concatenate([jnp.where(both, minus_upper, upper), jnp.where(both, minus_lower, lower)], axis=0)
+        kept = jnp.where((whole >= at) & (whole < at + 2 * PB), 0.0, s_ref[...])
         s_ref[...] = kept - cross(source, fresh)
-
-    def step(k, carry):
-        panel, before, done = carry
-        at = pl.multiple_of(k * PB, PB)
-        after = pl.multiple_of(((k + 1) % steps) * PB, PB)
-        cols = columns_of(panel, at, width)
-        inside = (lanes >= at) & (lanes < at + PB)
-        source = jnp.where(inside, jnp.where(lanes == at + rows, -1.0, 0.0), panel)
-        parts = [
-            [source[8 * g : 8 * g + 8, w * width : (w + 1) * width] for g in range(PB // 8)]
-            for w in range(size // width)
-        ]
-        update(at - PB, before, done)
-        following = s_ref[pl.ds(after, PB), :]
-        factors = columns_of(following, at, width)
-        parts = eliminate(cols, parts, width)
-        fresh = jnp.concatenate([jnp.concatenate(part, axis=0) for part in parts], axis=1)
-        s_ref[pl.ds(at, PB), :] = jnp.zeros((PB, size), F32)
-        following = jnp.where(inside, 0.0, following)
-        parts = [
-            [following[8 * g : 8 * g + 8, w * width : (w + 1) * width] for g in range(PB // 8)]
-            for w in range(size // width)
-        ]
-        for w in range(size // width):
-            for l in range(PB):
-                line = jnp.broadcast_to(fresh[l : l + 1, w * width : (w + 1) * width], (8, width))
-                for g in range(PB // 8):
-                    parts[w][g] = parts[w][g] - factors[l][g] * line
-        following = jnp.concatenate([jnp.concatenate(part, axis=0) for part in parts], axis=1)
-        return following, source, fresh
-
-    blank = jnp.zeros((PB, size), F32)
-    carry = (s_ref[0:PB, :], blank, blank)
+        s_ref[pl.ds(at, 2 * PB), :] = fresh
+        return carry
+
     start = 0
     for end, action in between:
-        carry = lax.fori_loop(start, end, step, carry)
+        lax.fori_loop(start, end, step, 0)
         action()
         start = end
-    _, before, done = lax.fori_loop(start, steps, step, carry)
-    update(size - PB, before, done)
+    lax.fori_loop(start, steps, step, 0)
 
 
 def dot(a, b):
@@ -344,8 +351,8 @@
         merge(s)
 
     each(CHUNKS - 1, go)
+    gram_3(0)
     merge(CHUNKS - 1)
-    gram_3(0)
 
     def e1_copy(to):
         return send(own, m_all.at[p], e1_s.at[0], e1_r.at[q // group], (z, to))
@@ -370,9 +377,11 @@
         gram_1(1, own, m_all.at[other])
         round_q(lambda to: e1_copy(2 * to + c).start())
 
+    moments_a()
+    share_moments()
     gram_4(0)
     inverse[...] = system_of(gram_5(0))
-    sweep(inverse, ((EARLY, moments_a), (EARLY + 2, share_moments)))
+    sweep(inverse, ((MIDDLE, lambda: gram_2(1)),))
     fa_ref[...] = -full_dot(own[...], inverse[...])
 
     def group_of(s):
@@ -407,7 +416,9 @@
         size = high // CHUNKS
         at = pl.multiple_of(x * size, size)
         block = m_all[pl.ds(x * 2 * group, 2 * group)].reshape(size, rank)
-        ah, al = split2(-full_dot(block, inverse[...]).T)
+        mh, ml = split2(block)
+        ih, il = split2(inverse[...])
+        ah, al = split2(-(dot(mh, ih) + dot(ml, ih) + dot(mh, il)).T)
         for n in range(2):
             part = total_b[n]
             for m in range(layers // 2):
@@ -420,13 +431,12 @@
 
     total_b[...] = jnp.zeros_like(total_b)
     forward(0)
-    gram_2(1)
 
     def go_back(s):
         forward(s + 1)
         back(s)
 
-        @pl.when(s == 1)
+        @pl.when(s == 0)
         def _():
             gram_3(1)
 

time: 70.2 us -> 63.7 us (0.907)
  Pallas kernels: 66.7 us -> 60.2 us
    pallas_call x1, Pallas kernels: 66.7 us -> 60.2 us  [local(): pl.pallas_call(functools.partial(kernel, nz, nj), out_shape=(out, out), i...]
where the time goes in v3:
time: 63.7 us; the launch traced here: 63.5 us
  Pallas kernels  60.2 us (95%)
  local copies, waits for them, and re-layouts  2.68 us (4%)
  between operations  0.65 us (1%)
    pallas_call x1, Pallas kernels, local(): pl.pallas_call(functools.partial(kernel, nz, nj), out_shape=(out, out), i...  60.2 us
    unnamed x6, local copies, waits for them, and re-layouts  2.68 us

profile of v3, /device:TPU:1, one launch (start us, length us, event | category | flops | bytes accessed | tf_op | source)
XLA Modules:
  0.0 63.5 jit_solution(9389617365768855201)
XLA Ops:
  0.6 0.0 copy-start
  0.6 0.7 %copy-done = f32[32,256]{1,0:T(8,128)S(1)} copy-done((f32[32,256]{1,0:T(8,128)S(1)}, f32[32,256]{1,0:T(8,128)}, u32[]{:S(2)}) %copy-start) | copy-done | bytes 32792
  1.4 0.0 copy-start.1
  1.4 0.7 %copy-done.1 = f32[8,256]{1,0:T(8,128)S(1)} copy-done((f32[8,256]{1,0:T(8,128)S(1)}, f32[8,256]{1,0:T(8,128)}, u32[]{:S(2)}) %copy-start.1) | copy-done | bytes 8216
  2.1 60.2 %shard_map.50 = (f32[32,256]{1,0:T(8,128)S(1)}, f32[32,256]{1,0:T(8,128)S(1)}) custom-call(f32[8,1024,256]{2,1,0:T(8,128)} %t_hbm.1, f32[32,256]{1,0:T(8,128)S(1)} %copy-done, f32[8,256]{1,0:T(8,128)S(1)} %copy-done.1), custom_call_target="tpu_custom_call" | custom-call | flops 2147483648 | bytes 8388608 | tf_op jit(solution)/shard_map/pallas_call | solution.py:494
  62.3 0.6 copy.7
  62.9 0.6 copy.8
Async XLA Ops:
  0.6 0.8 %copy-start = (f32[32,256]{1,0:T(8,128)S(1)}, f32[32,256]{1,0:T(8,128)}, u32[]{:S(2)}) copy-start(f32[32,256]{1,0:T(8,128)} %b_hbm.1) | copy-start | bytes 98308
  1.4 0.7 %copy-start.1 = (f32[8,256]{1,0:T(8,128)S(1)}, f32[8,256]{1,0:T(8,128)}, u32[]{:S(2)}) copy-start(f32[8,256]{1,0:T(8,128)} %c_hbm.1) | copy-start | bytes 24580

commit v4 on v3

--- a/solution.py
+++ b/solution.py
@@ -13,7 +13,7 @@
 BF16 = jnp.bfloat16
 PB = 16
 CHUNKS = 4
-MIDDLE = 5
+MIDDLE = 6
 
 
 def split2(x):
@@ -143,7 +143,7 @@
     return jnp.dot(a, b, precision=lax.Precision.HIGHEST, preferred_element_type=F32)
 
 
-def kernel(nz, nj, t_hbm, b_hbm, c_hbm, fa_ref, fb_ref,
+def kernel(nz, nj, t_hbm, bc_hbm, fa_ref, fb_ref,
            t_f32, t_hi, t_lo, w_hi, w_lo, b_all, b_sib, c_v, c_pad, c_turn, gram_c,
            gram, g1, g1_sum, g2, g2_sum, g3, inverse, system,
            tot, sib, comb, landed, own, m_all, total_b, tot_b, h_land,
@@ -183,8 +183,8 @@
     round_z(lambda to: pl.semaphore_signal(barrier, inc=1, device_id=(to, p), device_id_type=MESH))
     pl.semaphore_signal(barrier, inc=1, device_id=(z, other), device_id_type=MESH)
 
-    b_copy = pltpu.make_async_copy(b_hbm, b_all.at[z], in_sem.at[0])
-    c_copy = pltpu.make_async_copy(c_hbm, c_v, in_sem.at[1])
+    b_copy = pltpu.make_async_copy(bc_hbm.at[pl.ds(0, per)], b_all.at[z], in_sem.at[0])
+    c_copy = pltpu.make_async_copy(bc_hbm.at[pl.ds(per, layers)], c_v, in_sem.at[1])
     b_copy.start()
     c_copy.start()
     t_copies = [pltpu.make_async_copy(t_hbm.at[k], t_f32.at[k], t_sem.at[k]) for k in range(layers)]
@@ -382,7 +382,6 @@
     gram_4(0)
     inverse[...] = system_of(gram_5(0))
     sweep(inverse, ((MIDDLE, lambda: gram_2(1)),))
-    fa_ref[...] = -full_dot(own[...], inverse[...])
 
     def group_of(s):
         return (q // group + s + s // 2 - 2 * (s // 3)) % CHUNKS
@@ -451,6 +450,7 @@
 
     round_z(lambda to: h_copy(to, z).start())
     gram_4(1)
+    fa_ref[...] = -full_dot(own[...], inverse[...])
     h_land[z] = tot_b[z]
 
     system[...] = full_dot(inverse[...], gram_5(1))
@@ -494,7 +494,7 @@
         return pl.pallas_call(
             functools.partial(kernel, nz, nj),
             out_shape=(out, out),
-            in_specs=[anywhere] * 3,
+            in_specs=[anywhere] * 2,
             out_specs=(whole, whole),
             scratch_shapes=[
                 vm((layers, high, wide), F32),
@@ -519,7 +519,7 @@
             cost_estimate=pl.CostEstimate(
                 flops=4 * layers * high * wide * rank, bytes_accessed=4 * layers * high * wide, transcendentals=0
             ),
-        )(tensor, factor_b, factor_c)
+        )(tensor, jnp.concatenate([factor_b, factor_c], axis=0))
 
     in_specs = (P(None, "ia", "ja"), P(("ja", "ia"), None), P())
     out_specs = (P(("ia", "ja"), None), P(("ja", "ia"), None))

time: 63.7 us -> 62.7 us (0.984)
  local copies, waits for them, and re-layouts: 2.68 us -> 1.23 us
  other arithmetic: 0 us -> 0.78 us
    unnamed x6 -> x2, local copies, waits for them, and re-layouts: 2.68 us -> 1.23 us
    concatenate x0 -> x1, other arithmetic: none -> 0.78 us  [local(): jnp.concatenate([factor_b, factor_c], axis=0)]
where the time goes in v4:
time: 62.7 us; the launch traced here: 62.5 us
  Pallas kernels  59.9 us (96%)
  local copies, waits for them, and re-layouts  1.23 us (2%)
  other arithmetic  0.78 us (1%)
  between operations  0.64 us (1%)
    pallas_call x1, Pallas kernels, local(): pl.pallas_call(functools.partial(kernel, nz, nj), out_shape=(out, out), i...  59.9 us

profile of v4, /device:TPU:1, one launch (start us, length us, event | category | flops | bytes accessed | tf_op | source)
XLA Modules:
  0.0 62.5 jit_solution(14304675004969728061)
XLA Ops:
  0.6 0.8 %pad_maximum_fusion.bc_hbm = f32[40,256]{1,0:T(8,128)S(1)} fusion(f32[8,256]{1,0:T(8,128)} %param.5, f32[32,256]{1,0:T(8,128)} %param.4), kind=kLoop, calls=%fused_computation | loop fusion | flops 10240 | bytes 81920 | tf_op jit(solution)/shard_map/concatenate | solution.py:522
  1.4 59.9 %shard_map.50 = (f32[32,256]{1,0:T(8,128)S(1)}, f32[32,256]{1,0:T(8,128)S(1)}) custom-call(f32[8,1024,256]{2,1,0:T(8,128)} %t_hbm.1, f32[40,256]{1,0:T(8,128)S(1)} %pad_maximum_fusion.bc_hbm), custom_call_target="tpu_custom_call" | custom-call | flops 2147483648 | bytes 8388608 | tf_op jit(solution)/shard_map/pallas_call | solution.py:494
  61.3 0.6 copy.7
  61.9 0.6 copy.8

commit v5 on v4

--- a/solution.py
+++ b/solution.py
@@ -169,14 +169,16 @@
         lax.fori_loop(0, n, lambda s, carry: (body(s), carry)[1], 0)
 
     def round_z(body):
-        each(nz - 1, lambda s: body((z + 1 + (s + nz // 2 - 1) % (nz - 1)) % nz))
+        for s in range(nz - 1):
+            body((z + 1 + (s + nz // 2 - 1) % (nz - 1)) % nz)
 
     def round_half(n, body):
         each(nz // 2 - 1, lambda s: body(n * (nz // 2) + (z + 1 + s) % (nz // 2)))
 
     def round_q(body):
         far = (nq // 2 + nq // 8 - 1) % (nq - 1)
-        each(nq - 1, lambda s: body((q + 1 + (s + far) % (nq - 1)) % nq))
+        for s in range(nq - 1):
+            body((q + 1 + (s + far) % (nq - 1)) % nq)
 
     barrier = pltpu.get_barrier_semaphore()
     round_q(lambda to: pl.semaphore_signal(barrier, inc=1, device_id=(z, 2 * to + c), device_id_type=MESH))
@@ -378,8 +380,8 @@
         round_q(lambda to: e1_copy(2 * to + c).start())
 
     moments_a()
+    gram_4(0)
     share_moments()
-    gram_4(0)
     inverse[...] = system_of(gram_5(0))
     sweep(inverse, ((MIDDLE, lambda: gram_2(1)),))
 

time: 62.7 us -> 62.1 us (level)
  no operation moved by 1% of the time
where the time goes in v5:
time: 62.1 us; the launch traced here: 62 us
  Pallas kernels  59.3 us (95%)
  local copies, waits for them, and re-layouts  1.23 us (2%)
  other arithmetic  0.78 us (1%)
  between operations  0.64 us (1%)
    pallas_call x1, Pallas kernels, local(): pl.pallas_call(functools.partial(kernel, nz, nj), out_shape=(out, out), i...  59.3 us

profile of v5, /device:TPU:1, one launch (start us, length us, event | category | flops | bytes accessed | tf_op | source)
XLA Modules:
  0.0 62.0 jit_solution(3888011206915646769)
XLA Ops:
  0.6 0.8 %pad_maximum_fusion.bc_hbm = f32[40,256]{1,0:T(8,128)S(1)} fusion(f32[8,256]{1,0:T(8,128)} %param.5, f32[32,256]{1,0:T(8,128)} %param.4), kind=kLoop, calls=%fused_computation | loop fusion | flops 10240 | bytes 81920 | tf_op jit(solution)/shard_map/concatenate | solution.py:524
  1.4 59.3 %shard_map.50 = (f32[32,256]{1,0:T(8,128)S(1)}, f32[32,256]{1,0:T(8,128)S(1)}) custom-call(f32[8,1024,256]{2,1,0:T(8,128)} %t_hbm.1, f32[40,256]{1,0:T(8,128)S(1)} %pad_maximum_fusion.bc_hbm), custom_call_target="tpu_custom_call" | custom-call | flops 2147483648 | bytes 8388608 | tf_op jit(solution)/shard_map/pallas_call | solution.py:496
  60.8 0.6 copy.7
  61.4 0.6 copy.8

commit v6 on v5

--- a/solution.py
+++ b/solution.py
@@ -435,11 +435,12 @@
 
     def go_back(s):
         forward(s + 1)
-        back(s)
 
         @pl.when(s == 0)
         def _():
             gram_3(1)
+
+        back(s)
 
     each(CHUNKS - 1, go_back)
     back(CHUNKS - 1)

time: 62.1 us -> 62.7 us (level)
  no operation moved by 1% of the time
where the time goes in v6:
time: 62.7 us; the launch traced here: 62.5 us
  Pallas kernels  59.9 us (96%)
  local copies, waits for them, and re-layouts  1.23 us (2%)
  other arithmetic  0.78 us (1%)
  between operations  0.64 us (1%)
    pallas_call x1, Pallas kernels, local(): pl.pallas_call(functools.partial(kernel, nz, nj), out_shape=(out, out), i...  59.9 us

profile of v6, /device:TPU:1, one launch (start us, length us, event | category | flops | bytes accessed | tf_op | source)
XLA Modules:
  0.0 62.5 jit_solution(17427289250368536985)
XLA Ops:
  0.6 0.8 %pad_maximum_fusion.bc_hbm = f32[40,256]{1,0:T(8,128)S(1)} fusion(f32[8,256]{1,0:T(8,128)} %param.5, f32[32,256]{1,0:T(8,128)} %param.4), kind=kLoop, calls=%fused_computation | loop fusion | flops 10240 | bytes 81920 | tf_op jit(solution)/shard_map/concatenate | solution.py:525
  1.4 59.9 %shard_map.50 = (f32[32,256]{1,0:T(8,128)S(1)}, f32[32,256]{1,0:T(8,128)S(1)}) custom-call(f32[8,1024,256]{2,1,0:T(8,128)} %t_hbm.1, f32[40,256]{1,0:T(8,128)S(1)} %pad_maximum_fusion.bc_hbm), custom_call_target="tpu_custom_call" | custom-call | flops 2147483648 | bytes 8388608 | tf_op jit(solution)/shard_map/pallas_call | solution.py:497
  61.3 0.6 copy.7
  61.9 0.6 copy.8
